TPU v7x, 32 devices: a whole 2x2x4 slice. The times are simulated.
32 devices in a mesh: src: 8 (over z, core), loop: 4 (over y, x).
Axes of the slice: x: 2, y: 2, z: 4, core: 2. Of those that a mesh axis runs over, the one named last changes fastest.
Arguments:
- sources: bfloat16 [16384, 768], P(('src', 'loop')), may hold values from -48 to 48
- log_a: float32 [16384], P(('src', 'loop')), may hold values from -3 to 0
- targets: bfloat16 [64, 512, 768], P('src'), may hold values from -6 to 6
- g_old: bfloat16 [64, 512], P('src'), may hold values from -2.5 to 2.5
- log_b: float32 [64, 512], P('src'), may hold values from -3 to 0
- tile_ids: int32 [32, 8, 2], P(('src', 'loop')), may hold values from 0 to 63, as said below
- live_count: int32 [32, 8], P(('src', 'loop')), may hold values from 1 to 2, as said below
Outputs:
- f_new: float32 [16384], P(('src', 'loop'))
- g_new: float32 [64, 512], P('src')
Inputs may be any that keep to these rules, and one draw needn't show every extreme that they name: `tile_ids`: tile ids of one device for index o of src lie in o * 8 to (o + 1) * 8 - 1 and are distinct within that group of 2 slots; every tile is in use in some device's list. `live_count`: every index of src has a full group of 2 slots in use in some device's list.
All inputs are finite; a program needn't handle non-finite values.
Results may differ from a plain program's by a relative error of at most 0.0003.
Values may be sent and summed in bfloat16 or wider, within the bound.
A program may use at most 128 MiB of HBM per device.

v0:
```python
import math

import jax
import jax.numpy as jnp
from jax import lax
from jax.sharding import PartitionSpec as P

EPSILON = 0.1
VERY_LOW = -1e30


def combined_all(part, axis, combine):
    gathered = jax.tree.map(lambda a: lax.all_gather(a, axis), part)

    def take(source):
        return jax.tree.map(lambda a: lax.dynamic_index_in_dim(a, source, 0, False), gathered)

    return lax.fori_loop(
        1, lax.axis_size(axis), lambda source, state: combine(state, take(source)), take(0)
    )


def similarity(rows_bf, fetched):
    kernel = jnp.einsum("rd,ctd->rct", rows_bf, fetched, preferred_element_type=jnp.float32)
    return kernel / math.sqrt(rows_bf.shape[1])


def row_part(rows_bf, fetched, potential, live_slots):
    kernel = similarity(rows_bf, fetched)
    logits = (potential.astype(jnp.float32)[None] + kernel) / EPSILON
    logits = jnp.where(live_slots[None, :, None], logits, VERY_LOW)
    top = jnp.max(logits, axis=(1, 2))
    total = jnp.sum(jnp.exp(logits - top[:, None, None]), axis=(1, 2))
    return (top, total)


def col_part(rows_bf, row_potential, fetched, live_slots):
    kernel = similarity(rows_bf, fetched)
    logits = (row_potential[:, None, None] + kernel) / EPSILON
    top = jnp.max(logits, axis=0)
    total = jnp.sum(jnp.exp(logits - top[None]), axis=0)
    top = jnp.where(live_slots[:, None], top, VERY_LOW)
    total = jnp.where(live_slots[:, None], total, 0.0)
    return (top, total)


def combine(first, second):
    top = jnp.maximum(first[0], second[0])
    total = first[1] * jnp.exp(first[0] - top) + second[1] * jnp.exp(second[0] - top)
    return (top, total)


def fold_rows(row_top, row_total):
    top = jnp.max(row_top, axis=0)
    total = jnp.sum(row_total * jnp.exp(row_top - top[None]), axis=0)
    return (top, total)


def local(sources, log_a, targets, g_old, log_b, tile_ids, live_count):
    tiles_own = targets.shape[0]
    width = targets.shape[1]
    slots_per = tile_ids.shape[2]
    requested = tile_ids[0]
    live_slots = jnp.arange(slots_per, dtype=jnp.int32)[None, :] < live_count[0][:, None]
    base_id = lax.axis_index("src") * tiles_own
    arrived = lax.all_to_all(requested, "src", split_axis=0, concat_axis=0, tiled=True)
    local_ids = arrived - base_id
    packed = targets[local_ids]
    packed_pot = g_old[local_ids]
    fetched, fetched_pot = (
        lax.all_to_all(packed, "src", split_axis=0, concat_axis=0, tiled=True),
        lax.all_to_all(packed_pot, "src", split_axis=0, concat_axis=0, tiled=True),
    )

    def rows_of(item):
        return row_part(sources, item[0], item[1], item[2])

    row_top, row_total = lax.map(rows_of, (fetched, fetched_pot, live_slots))
    top, total = fold_rows(row_top, row_total)
    f_new = EPSILON * log_a - EPSILON * (top + jnp.log(total))

    def cols_of(item):
        return col_part(sources, f_new, item[0], item[1])

    col_top, col_total = lax.map(cols_of, (fetched, live_slots))
    col_top, col_total = (
        lax.all_to_all(col_top, "src", split_axis=0, concat_axis=0, tiled=True),
        lax.all_to_all(col_total, "src", split_axis=0, concat_axis=0, tiled=True),
    )
    flat_ids = local_ids.reshape(-1)
    flat_top = col_top.reshape(-1, width)
    flat_total = col_total.reshape(-1, width)
    onehot = flat_ids[:, None] == jnp.arange(tiles_own, dtype=jnp.int32)[None, :]
    tile_top = jnp.max(jnp.where(onehot[:, :, None], flat_top[:, None, :], VERY_LOW), axis=0)
    scaled = flat_total[:, None, :] * jnp.exp(
        jnp.minimum(flat_top[:, None, :] - tile_top[None], 0.0)
    )
    tile_total = jnp.sum(jnp.where(onehot[:, :, None], scaled, 0.0), axis=0)
    tile_top, tile_total = combined_all((tile_top, tile_total), "loop", combine)
    g_new = EPSILON * log_b - EPSILON * (tile_top + jnp.log(tile_total))
    return (f_new, g_new)


def solution(mesh):
    return jax.shard_map(
        local,
        mesh=mesh,
        in_specs=(
            P(("src", "loop"), None),
            P(("src", "loop")),
            P("src", None, None),
            P("src", None),
            P("src", None),
            P(("src", "loop"), None, None),
            P(("src", "loop"), None),
        ),
        out_specs=(P(("src", "loop")), P("src", None)),
        check_vma=False,
    )
```

profile of v0, /device:TPU:0, one launch (start us, length us, event | category | flops | bytes accessed | tf_op | source)
XLA Modules:
  0.0 392.4 jit_solution(17931586311628515938)
XLA Ops:
  0.6 1.4 copy.16
  2.0 6.3 %all-to-all-start = ((s32[8,1,2]{2,1,0:T(1,128)}), s32[8,1,2]{2,1,0:T(1,128)S(1)}, u32[]{:S(2)}, u32[]{:S(2)}) async-start(s32[8,1,2]{2,1,0:T(1,128)} %copy.16), calls=%async_computation | async-start | bytes 8192 | tf_op jit(solution)/shard_map/all_to_all | solution.py:66
  8.3 5.5 %all-to-all-done = s32[8,1,2]{2,1,0:T(1,128)S(1)} async-done(((s32[8,1,2]{2,1,0:T(1,128)}), s32[8,1,2]{2,1,0:T(1,128)S(1)}, u32[]{:S(2)}, u32[]{:S(2)}) %all-to-all-start) | async-done | bytes 96 | tf_op jit(solution)/shard_map/all_to_all | solution.py:66
  16.5 3.3 all-to-all-start.1
  19.8 9.2 %gather_fusion.1 = bf16[16,512,768]{2,1,0:T(8,128)(2,1)} fusion(bf16[8,512,768]{2,1,0:T(8,128)(2,1)} %param.15, s32[1024]{0:T(1024)S(1)} %pad_clamp_fusion), kind=kCustom, calls=%fused_computation.1 | custom fusion | bytes 25165888 | tf_op jit(solution)/shard_map/gather | solution.py:68
  29.0 5.5 %all-to-all-start.2 = ((bf16[8,2,512,768]{3,2,1,0:T(8,128)(2,1)}), bf16[8,2,512,768]{3,2,1,0:T(8,128)(2,1)}, u32[]{:S(2)}, u32[]{:S(2)}) async-start(bf16[8,2,512,768]{3,2,1,0:T(8,128)(2,1)} %bitcast.91), calls=%async_computation.2 | async-start | bytes 25165824 | tf_op jit(solution)/shard_map/all_to_all | solution.py:71
  34.7 273.6 %all-to-all-done.2 = bf16[8,2,512,768]{3,2,1,0:T(8,128)(2,1)} async-done(((bf16[8,2,512,768]{3,2,1,0:T(8,128)(2,1)}), bf16[8,2,512,768]{3,2,1,0:T(8,128)(2,1)}, u32[]{:S(2)}, u32[]{:S(2)}) %all-to-all-start.2) | async-done | bytes 12582944 | tf_op jit(solution)/shard_map/all_to_all | solution.py:71
  308.3 24.6 %while.41 = (s32[]{:T(128)}, f32[8,512]{1,0:T(8,128)S(1)}, f32[8,512]{1,0:T(8,128)S(1)}, pred[8,2]{1,0:T(8,128)(4,1)S(1)}, bf16[8,2,512]{2,1,0:T(2,128)(2,1)S(1)...) while((s32[]{:T(128)}, f32[8,512]{1,0:T(8,128)S(1)}, ...), condition=%wide.region_3.4_spmd, body=%wide.region_0.3_spmd.sunk | while | flops 808976384 | bytes 6578803 | solution.py:78
  308.3 2.5 fusion.21
  311.4 2.5 fusion.21
  314.5 2.5 fusion.21
  317.6 2.5 fusion.21
  320.7 2.5 fusion.21
  323.7 2.5 fusion.21
  326.8 2.5 fusion.21
  329.9 2.5 fusion.21
  333.0 29.6 %while.42 = (s32[]{:T(128)}, f32[8,2,512]{2,1,0:T(2,128)}, f32[8,2,512]{2,1,0:T(2,128)}, pred[8,2]{1,0:T(8,128)(4,1)S(1)}, f32[512]{0:T(512)S(1)}, /*index=5*/bf...) while((s32[]{:T(128)}, f32[8,2,512]{2,1,0:T(2,128)}, f32[8,2,512]{2,1,0:T(2,128)}, ...), condition=%wide.region_9.10_spmd, body=%wide.region_6.9_spmd.sunk | while | flops 810024960 | bytes 6587487 | solution.py:85
  333.1 2.4 bitcast_reduce_fusion.2
  336.8 2.4 bitcast_reduce_fusion.2
  340.4 2.4 bitcast_reduce_fusion.2
  344.1 2.4 bitcast_reduce_fusion.2
  347.8 2.4 bitcast_reduce_fusion.2
  350.9 0.7 fusion.23
  351.5 2.4 bitcast_reduce_fusion.2
  355.2 2.4 bitcast_reduce_fusion.2
  358.9 2.4 bitcast_reduce_fusion.2
  361.9 0.7 fusion.23
  362.6 3.3 all-to-all-start.3
  366.0 5.6 %all-to-all-done.3 = f32[8,2,512]{2,1,0:T(2,128)S(1)} async-done(((f32[8,2,512]{2,1,0:T(2,128)}), f32[8,2,512]{2,1,0:T(2,128)S(1)}, u32[]{:S(2)}, u32[]{:S(2)}) %all-to-all-start.3) | async-done | bytes 32800 | tf_op jit(solution)/shard_map/all_to_all | solution.py:87
  371.6 3.3 all-to-all-start.4
  375.1 8.2 %all-gather = f32[32,512]{1,0:T(8,128)S(1)} all-gather(f32[8,512]{1,0:T(8,128)S(1)} %select_reduce_fusion.1), channel_id=2, replica_groups=mesh['src'=8,'loop'=4] {'loop'}, dimensions={0}, use_global_device_ids=true | all-gather | bytes 81920 | tf_op jit(solution)/shard_map/all_gather | solution.py:13
  383.5 8.1 %all-gather.1 = f32[32,512]{1,0:T(8,128)S(1)} all-gather(f32[8,512]{1,0:T(8,128)S(1)} %select_reduce_fusion), channel_id=3, replica_groups=mesh['src'=8,'loop'=4] {'loop'}, dimensions={0}, use_global_device_ids=true | all-gather | bytes 81920 | tf_op jit(solution)/shard_map/all_gather | solution.py:13
  (106 shorter events, 16.6 us)
Async XLA Ops:
  0.6 14.6 %copy-start = (bf16[8,512]{1,0:T(8,128)(2,1)S(1)}, bf16[8,512]{1,0:T(8,128)(2,1)}, u32[]{:S(2)}) copy-start(bf16[8,512]{1,0:T(8,128)(2,1)} %param.16) | copy-start | bytes 24580
  2.0 11.8 %all-to-all-start = ((s32[8,1,2]{2,1,0:T(1,128)}), s32[8,1,2]{2,1,0:T(1,128)S(1)}, u32[]{:S(2)}, u32[]{:S(2)}) async-start(s32[8,1,2]{2,1,0:T(1,128)} %copy.16), calls=%async_computation | async-start | bytes 8192 | tf_op jit(solution)/shard_map/all_to_all | solution.py:66
  16.5 12.6 %all-to-all-start.1 = ((bf16[8,2,512]{2,1,0:T(2,128)(2,1)}), bf16[8,2,512]{2,1,0:T(2,128)(2,1)S(1)}, u32[]{:S(2)}, u32[]{:S(2)}) async-start(bf16[8,2,512]{2,1,0:T(2,128)(2,1)} %reshape.131), calls=%async_computation.1 | async-start | bytes 32768 | tf_op jit(solution)/shard_map/all_to_all | solution.py:72
  29.0 5.5 %copy-start.5 = (s32[1,8]{1,0:T(1,128)S(1)}, s32[1,8]{1,0:T(1,128)}, u32[]{:S(2)}) copy-start(s32[1,8]{1,0:T(1,128)} %param.19) | copy-start | bytes 100
  29.0 279.3 %copy-start.4 = (bf16[512,768]{1,0:T(8,128)(2,1)S(1)}, bf16[512,768]{1,0:T(8,128)(2,1)}, u32[]{:S(2)}) copy-start(bf16[512,768]{1,0:T(8,128)(2,1)} %param.13) | copy-start | bytes 2359300
  29.0 279.3 %all-to-all-start.2 = ((bf16[8,2,512,768]{3,2,1,0:T(8,128)(2,1)}), bf16[8,2,512,768]{3,2,1,0:T(8,128)(2,1)}, u32[]{:S(2)}, u32[]{:S(2)}) async-start(bf16[8,2,512,768]{3,2,1,0:T(8,128)(2,1)} %bitcast.91), calls=%async_computation.2 | async-start | bytes 25165824 | tf_op jit(solution)/shard_map/all_to_all | solution.py:71
  308.3 24.7 %copy-start.3 = (f32[512]{0:T(512)S(1)}, f32[512]{0:T(512)}, u32[]{:S(2)}) copy-start(f32[512]{0:T(512)} %param.14) | copy-start | bytes 6148
  333.0 58.8 %copy-start.2 = (f32[8,512]{1,0:T(8,128)S(1)}, f32[8,512]{1,0:T(8,128)}, u32[]{:S(2)}) copy-start(f32[8,512]{1,0:T(8,128)} %param.17) | copy-start | bytes 49156
  362.6 29.8 %copy-start.1 = (f32[512]{0:T(512)}, f32[512]{0:T(512)S(1)}, u32[]{:S(2)}) copy-start(f32[512]{0:T(512)S(1)} %get-tuple-element.477) | copy-start | bytes 6148
  362.6 9.0 %all-to-all-start.3 = ((f32[8,2,512]{2,1,0:T(2,128)}), f32[8,2,512]{2,1,0:T(2,128)S(1)}, u32[]{:S(2)}, u32[]{:S(2)}) async-start(f32[8,2,512]{2,1,0:T(2,128)} %get-tuple-element.213), calls=%async_computation.3 | async-start | bytes 65536 | tf_op jit(solution)/shard_map/all_to_all | solution.py:87
  371.6 11.7 %all-to-all-start.4 = ((f32[8,2,512]{2,1,0:T(2,128)}), f32[8,2,512]{2,1,0:T(2,128)S(1)}, u32[]{:S(2)}, u32[]{:S(2)}) async-start(f32[8,2,512]{2,1,0:T(2,128)} %get-tuple-element.214), calls=%async_computation.4 | async-start | bytes 65536 | tf_op jit(solution)/shard_map/all_to_all | solution.py:88
where the time goes:
time: 393 us; the launch traced here: 392 us
  waiting for transfers between devices  285 us (73%)
  matrix products  39.8 us (10%)
  starting transfers between devices  21.8 us (6%)
  blocking collectives  16.4 us (4%)
  other arithmetic  14.6 us (4%)
  local copies, waits for them, and re-layouts  13.8 us (4%)
    all_to_all x1, waiting for transfers between devices, local(): lax.all_to_all(packed, 'src', split_axis=0, concat_axis=0, tiled=True)  274 us
    dot_general x16, matrix products, similarity(): jnp.einsum('rd,ctd->rct', rows_bf, fetched, preferred_element_type=jnp.fl...  39.8 us
    all_gather x2, blocking collectives, combined_all(): gathered = jax.tree.map(lambda a: lax.all_gather(a, axis), part)  16.4 us
    gather x1, local copies, waits for them, and re-layouts, local(): packed = targets[local_ids]  9.21 us
  transfers between devices with their start and end apart: 5, of which 3 were waited for; matrix products, arithmetic and copies ran while one was open for 2% of the time, Pallas kernels for 0%

commit v1 on v0

v1 whole, which is shorter than its diff:
```python
import functools
import math

import jax
import jax.numpy as jnp
from jax import lax
from jax.experimental import pallas as pl
from jax.experimental.pallas import tpu as pltpu
from jax.sharding import PartitionSpec as P

EPSILON = 0.1
VERY_LOW = -1e30
LOG2E = math.log2(math.e)
LN2 = math.log(2.0)
CHUNKS = 2
MESH = pl.DeviceIdType.MESH


def fused(
    n_src, n_loop, slots,
    src_ref, tgt_ref, log_a_ref, g_old_ref, log_b_ref, idpack_ref,
    f_ref, g_ref,
    gather, tiles, logits, gcol, ids_v, ids_s, row_out, row_in, f_all,
    col_top, col_sum, loop_out, loop_in,
    gs_send, gs_recv, id_send, id_recv, row_send, row_recv, f_send, f_recv,
    loop_send, loop_recv, loc_sem,
):
    rows, depth = src_ref.shape
    tiles_own, width, _ = tgt_ref.shape
    chunk = rows // CHUNKS
    n_chip = n_src // 2
    scale = LOG2E / (EPSILON * math.sqrt(depth))
    me = lax.axis_index("src")
    ml = lax.axis_index("loop")
    chip = me // 2
    core = me % 2
    sib = chip * 2 + (1 - core)

    def at_src(s):
        return (s, ml)

    def peer(k):
        return lax.rem(me + k, n_src)

    def loop_peer(k):
        return lax.rem(ml + k, n_loop)

    tile_copy = pltpu.make_async_copy(tgt_ref, tiles, loc_sem.at[0])
    own_copy = pltpu.make_async_copy(src_ref, gather.at[me], loc_sem.at[1])
    own_ids = pltpu.make_async_copy(idpack_ref.at[me], ids_v.at[me], loc_sem.at[2])
    tile_copy.start()
    own_copy.start()
    own_ids.start()

    barrier = pltpu.get_barrier_semaphore()
    for k in range(1, n_src):
        pl.semaphore_signal(barrier, inc=1, device_id=(peer(k), ml), device_id_type=MESH)
    for k in range(1, n_loop):
        pl.semaphore_signal(barrier, inc=1, device_id=(me, loop_peer(k)), device_id_type=MESH)
    pl.semaphore_wait(barrier, n_src - 1 + n_loop - 1)

    def id_copy(to, slot):
        return pltpu.make_async_remote_copy(
            src_ref=idpack_ref.at[to], dst_ref=ids_v.at[slot],
            send_sem=id_send.at[to], recv_sem=id_recv.at[slot],
            device_id=at_src(to), device_id_type=MESH,
        )

    for k in range(1, n_src):
        id_copy(peer(k), me).start()

    def own_send(ch, lane, to):
        part = pl.ds(ch * chunk, chunk)
        return pltpu.make_async_remote_copy(
            src_ref=src_ref.at[part], dst_ref=gather.at[me, part],
            send_sem=gs_send.at[me, ch, lane], recv_sem=gs_recv.at[me, ch],
            device_id=at_src(to), device_id_type=MESH,
        )

    def pass_on(block, ch, lane, to):
        part = pl.ds(ch * chunk, chunk)
        return pltpu.make_async_remote_copy(
            src_ref=gather.at[block, part], dst_ref=gather.at[block, part],
            send_sem=gs_send.at[block, ch, lane], recv_sem=gs_recv.at[block, ch],
            device_id=at_src(to), device_id_type=MESH,
        )

    up = lax.rem(me + 2, n_src)
    down = lax.rem(me + n_src - 2, n_src)
    has_up = chip < n_chip - 1
    has_down = chip > 0
    for ch in range(CHUNKS):
        @pl.when(has_up)
        def _():
            own_send(ch, 0, up).start()

        @pl.when(has_down)
        def _():
            own_send(ch, 1, down).start()

    for ch in range(CHUNKS):
        own_send(ch, 2, sib).start()

    def fill(t, carry):
        row = g_old_ref[t] * (LOG2E / EPSILON)
        gcol[t] = jnp.broadcast_to(row, (128, width)).T
        return carry

    lax.fori_loop(0, tiles_own, fill, 0)

    own_ids.wait()
    for k in range(1, n_src):
        id_copy(peer(k), peer(k)).wait_recv()
    to_smem = pltpu.make_async_copy(ids_v, ids_s, loc_sem.at[3])
    to_smem.start()
    to_smem.wait()
    tile_copy.wait()
    own_copy.wait()

    def row_copy(to, slot):
        return pltpu.make_async_remote_copy(
            src_ref=row_out.at[to], dst_ref=row_in.at[slot],
            send_sem=row_send.at[to], recv_sem=row_recv.at[slot],
            device_id=at_src(to), device_id_type=MESH,
        )

    def row_part(block, ch):
        part = pl.ds(pl.multiple_of(ch * chunk, chunk), chunk)
        rows_bf = gather[block, part, :]
        live = ids_s[block, 0, slots]
        best = None
        for c in range(slots):
            tid = ids_s[block, 0, c]
            dots = lax.dot_general(
                tiles[tid], rows_bf, (((1,), (1,)), ((), ())),
                preferred_element_type=jnp.float32,
            )
            g_rows = gcol[tid]
            vals = dots * scale + jnp.concatenate([g_rows] * (chunk // 128), axis=1)
            logits[block * slots + c, :, part] = vals
            top = jnp.max(vals, axis=0, keepdims=True)
            total = jnp.sum(jnp.exp2(vals - top), axis=0, keepdims=True)
            if c == 0:
                best, tot = top, total
            else:
                top = jnp.where(c < live, top, VERY_LOW)
                total = jnp.where(c < live, total, 0.0)
                new = jnp.maximum(best, top)
                tot = tot * jnp.exp2(best - new) + total * jnp.exp2(top - new)
                best = new
        row_out[block, 0:1, part] = best
        row_out[block, 1:2, part] = tot

    def own_step(ch, carry):
        row_part(me, ch)
        return carry

    lax.fori_loop(0, CHUNKS, own_step, 0)
    row_in[me] = row_out[me]

    def sib_step(ch, carry):
        pass_on(sib, ch, 2, sib).wait_recv()
        row_part(sib, ch)
        return carry

    lax.fori_loop(0, CHUNKS, sib_step, 0)
    row_copy(sib, me).start()

    def chip_step(k, carry):
        low = chip - k
        high = chip + k

        def chunk_step(ch, carry):
            @pl.when(low >= 0)
            def _():
                block = low * 2 + core
                pass_on(block, ch, 0, up).wait_recv()

                @pl.when(has_up)
                def _():
                    pass_on(block, ch, 0, up).start()

                pass_on(block, ch, 2, sib).start()

            @pl.when(high < n_chip)
            def _():
                block = high * 2 + core
                pass_on(block, ch, 1, down).wait_recv()

                @pl.when(has_down)
                def _():
                    pass_on(block, ch, 1, down).start()

                pass_on(block, ch, 2, sib).start()

            def part_step(j, carry):
                other = jnp.where(j % 2 == 0, low, high)
                own_core = j < 2

                @pl.when((other >= 0) & (other < n_chip))
                def _():
                    block = other * 2 + jnp.where(own_core, core, 1 - core)

                    @pl.when(jnp.logical_not(own_core))
                    def _():
                        pass_on(block, ch, 2, sib).wait_recv()

                    row_part(block, ch)

                    @pl.when(ch == CHUNKS - 1)
                    def _():
                        row_copy(block, me).start()

                return carry

            return lax.fori_loop(0, 4, part_step, carry)

        return lax.fori_loop(0, CHUNKS, chunk_step, carry)

    lax.fori_loop(1, n_chip, chip_step, 0)

    for k in range(1, n_src):
        row_copy(peer(k), peer(k)).wait_recv()
    tops = row_in[:, 0, :]
    best = jnp.max(tops, axis=0, keepdims=True)
    total = jnp.sum(row_in[:, 1, :] * jnp.exp2(tops - best), axis=0, keepdims=True)
    f_two = log_a_ref[...] * LOG2E - (best + jnp.log2(total))
    f_ref[...] = f_two * (EPSILON * LN2)
    f_all[me] = f_two

    def f_copy(to, slot):
        return pltpu.make_async_remote_copy(
            src_ref=f_all.at[slot], dst_ref=f_all.at[slot],
            send_sem=f_send.at[to], recv_sem=f_recv.at[slot],
            device_id=at_src(to), device_id_type=MESH,
        )

    for k in range(1, n_src):
        f_copy(peer(k), me).start()
    for k in range(1, n_src):
        f_copy(peer(k), peer(k)).wait_recv()

    n_pairs = n_src * slots
    band = 32
    lane = lax.broadcasted_iota(jnp.int32, (band, 128), 1)

    def band_step(r, carry):
        at = pl.ds(pl.multiple_of(r * band, band), band)

        def pair_step(p, state):
            tops, sums = state
            vals = logits[p, at, :] + f_all[p // slots]
            parts = [vals[:, i : i + 128] for i in range(0, rows, 128)]
            top = functools.reduce(jnp.maximum, parts)
            total = functools.reduce(jnp.add, [jnp.exp2(v - top) for v in parts])
            full = jnp.max(top, axis=1, keepdims=True)
            total = jnp.sum(total * jnp.exp2(top - full), axis=1, keepdims=True)
            return (jnp.where(lane == p, full, tops), jnp.where(lane == p, total, sums))

        zero = jnp.zeros((band, 128), jnp.float32)
        tops, sums = lax.fori_loop(0, n_pairs, pair_step, (zero, zero), unroll=4)
        col_top[at, :] = tops
        col_sum[at, :] = sums
        return carry

    lax.fori_loop(0, width // band, band_step, 0)
    tops = col_top[...].T
    sums = col_sum[...].T
    index = lax.broadcasted_iota(jnp.int32, (tiles_own, width), 0)
    masks = []
    tile_top = jnp.full((tiles_own, width), VERY_LOW, jnp.float32)
    for p in range(n_pairs):
        block, c = p // slots, p % slots
        tid = jnp.where(c < ids_s[block, 0, slots], ids_s[block, 0, c], -1)
        mask = index == tid
        masks.append(mask)
        tile_top = jnp.maximum(tile_top, jnp.where(mask, tops[p : p + 1], VERY_LOW))
    tile_sum = jnp.zeros((tiles_own, width), jnp.float32)
    for p in range(n_pairs):
        term = sums[p : p + 1] * jnp.exp2(jnp.minimum(tops[p : p + 1] - tile_top, 0.0))
        tile_sum = tile_sum + jnp.where(masks[p], term, 0.0)

    loop_in[ml, 0] = tile_top
    loop_in[ml, 1] = tile_sum
    loop_out[0] = tile_top
    loop_out[1] = tile_sum

    def loop_copy(to, slot):
        return pltpu.make_async_remote_copy(
            src_ref=loop_out, dst_ref=loop_in.at[slot],
            send_sem=loop_send.at[to], recv_sem=loop_recv.at[slot],
            device_id=(me, to), device_id_type=MESH,
        )

    for k in range(1, n_loop):
        loop_copy(loop_peer(k), ml).start()
    for k in range(1, n_loop):
        loop_copy(loop_peer(k), loop_peer(k)).wait_recv()
    top = functools.reduce(jnp.maximum, [loop_in[i, 0] for i in range(n_loop)])
    total = functools.reduce(
        jnp.add, [loop_in[i, 1] * jnp.exp2(loop_in[i, 0] - top) for i in range(n_loop)]
    )
    g_ref[...] = (
        EPSILON * log_b_ref[...] - (EPSILON * LN2) * (top + jnp.log2(total)) + g_old_ref[:, 0, :]
    )

    for k in range(1, n_loop):
        loop_copy(loop_peer(k), ml).wait_send()
    for k in range(1, n_src):
        f_copy(peer(k), me).wait_send()
        row_copy(peer(k), me).wait_send()
        id_copy(peer(k), me).wait_send()
    for ch in range(CHUNKS):
        @pl.when(has_up)
        def _():
            own_send(ch, 0, up).wait_send()

        @pl.when(has_down)
        def _():
            own_send(ch, 1, down).wait_send()

        own_send(ch, 2, sib).wait_send()

    def drain(k, carry):
        low = chip - k
        high = chip + k
        for ch in range(CHUNKS):
            @pl.when(low >= 0)
            def _():
                block = low * 2 + core

                @pl.when(has_up)
                def _():
                    pass_on(block, ch, 0, up).wait_send()

                pass_on(block, ch, 2, sib).wait_send()

            @pl.when(high < n_chip)
            def _():
                block = high * 2 + core

                @pl.when(has_down)
                def _():
                    pass_on(block, ch, 1, down).wait_send()

                pass_on(block, ch, 2, sib).wait_send()

        return carry

    lax.fori_loop(1, n_chip, drain, 0)


def local(sources, log_a, targets, g_old, log_b, tile_ids, live_count):
    n_src = lax.axis_size("src")
    n_loop = lax.axis_size("loop")
    rows, depth = sources.shape
    tiles_own, width = targets.shape[0], targets.shape[1]
    slots = tile_ids.shape[2]
    base = jnp.arange(n_src, dtype=jnp.int32) * tiles_own
    listed = jnp.concatenate([tile_ids[0] - base[:, None], live_count[0][:, None]], axis=1)
    idpack = jnp.pad(listed, ((0, 0), (0, 128 - slots - 1)))[:, None, :]
    vmem = pl.BlockSpec(memory_space=pltpu.VMEM)
    hbm = pl.BlockSpec(memory_space=pl.ANY)
    dma = pltpu.SemaphoreType.DMA
    n_pairs = n_src * slots
    f_new, g_new = pl.pallas_call(
        functools.partial(fused, n_src, n_loop, slots),
        out_shape=(
            jax.ShapeDtypeStruct((1, rows), jnp.float32),
            jax.ShapeDtypeStruct((tiles_own, width), jnp.float32),
        ),
        in_specs=[hbm, hbm, vmem, vmem, vmem, vmem],
        out_specs=(vmem, vmem),
        scratch_shapes=[
            pltpu.VMEM((n_src, rows, depth), sources.dtype),
            pltpu.VMEM((tiles_own, width, depth), targets.dtype),
            pltpu.VMEM((n_pairs, width, rows), jnp.float32),
            pltpu.VMEM((tiles_own, width, 128), jnp.float32),
            pltpu.VMEM((n_src, 1, 128), jnp.int32),
            pltpu.SMEM((n_src, 1, 128), jnp.int32),
            pltpu.VMEM((n_src, 2, rows), jnp.float32),
            pltpu.VMEM((n_src, 2, rows), jnp.float32),
            pltpu.VMEM((n_src, 1, rows), jnp.float32),
            pltpu.VMEM((width, 128), jnp.float32),
            pltpu.VMEM((width, 128), jnp.float32),
            pltpu.VMEM((2, tiles_own, width), jnp.float32),
            pltpu.VMEM((n_loop, 2, tiles_own, width), jnp.float32),
            dma((n_src, CHUNKS, 3)),
            dma((n_src, CHUNKS)),
            dma((n_src,)),
            dma((n_src,)),
            dma((n_src,)),
            dma((n_src,)),
            dma((n_src,)),
            dma((n_src,)),
            dma((n_loop,)),
            dma((n_loop,)),
            dma((4,)),
        ],
        compiler_params=pltpu.CompilerParams(
            collective_id=0, has_side_effects=True, vmem_limit_bytes=60 * 1024 * 1024
        ),
        cost_estimate=pl.CostEstimate(
            flops=2 * n_pairs * rows * width * depth,
            bytes_accessed=2 * (tiles_own * width + rows) * depth,
            transcendentals=2 * n_pairs * rows * width,
        ),
    )(
        sources,
        targets,
        log_a[None],
        g_old.astype(jnp.float32)[:, None, :],
        log_b,
        idpack,
    )
    return (f_new[0], g_new)


def solution(mesh):
    return jax.shard_map(
        local,
        mesh=mesh,
        in_specs=(
            P(("src", "loop"), None),
            P(("src", "loop")),
            P("src", None, None),
            P("src", None),
            P("src", None),
            P(("src", "loop"), None, None),
            P(("src", "loop"), None),
        ),
        out_specs=(P(("src", "loop")), P("src", None)),
        check_vma=False,
    )
```

time: 393 us -> 93.2 us (0.24)
  waiting for transfers between devices: 285 us -> 0 us
  Pallas kernels: 0 us -> 86 us
  matrix products: 39.8 us -> 0 us
  starting transfers between devices: 21.8 us -> 0 us
  blocking collectives: 16.4 us -> 0 us
  other arithmetic: 14.6 us -> 0.15 us
  local copies, waits for them, and re-layouts: 13.8 us -> 5.96 us
    all_to_all x5 -> x0, waiting for transfers between devices: 285 us -> none  [the longest x1 274 us: local(): lax.all_to_all(packed, 'src', split_axis=0, concat_axis=0, tiled=True)]
    pallas_call x0 -> x1, Pallas kernels: none -> 86 us  [local(): pl.pallas_call(functools.partial(fused, n_src, n_loop, slots), out_shape=...]
    dot_general x16 -> x0, matrix products: 39.8 us -> none  [similarity(): jnp.einsum('rd,ctd->rct', rows_bf, fetched, preferred_element_type=jnp.fl...]
    all_to_all x5 -> x0, starting transfers between devices: 21.8 us -> none  [the longest x1 6.33 us: local(): lax.all_to_all(requested, 'src', split_axis=0, concat_axis=0, tiled=True)]
    all_gather x2 -> x0, blocking collectives: 16.4 us -> none  [combined_all(): gathered = jax.tree.map(lambda a: lax.all_gather(a, axis), part)]
    gather x3 -> x0, local copies, waits for them, and re-layouts: 10.4 us -> none  [the longest x1 9.21 us: local(): packed = targets[local_ids]]
    reduce_sum x18 -> x0, other arithmetic: 7.46 us -> none  [the longest x8 4.45 us: col_part(): total = jnp.sum(jnp.exp(logits - top[None]), axis=0)]
    dynamic_update_slice x8 -> x0, other arithmetic: 5.4 us -> none  [local(): col_top, col_total = lax.map(cols_of, (fetched, live_slots))]
  transfers between devices with their start and end apart: 5 -> 0, of which waited for: 3 -> 0; matrix products, arithmetic and copies ran while one was open for 2% -> 0% of each run, Pallas kernels for 0% -> 0%
where the time goes in v1:
time: 93.2 us; the launch traced here: 92.8 us
  Pallas kernels  86 us (92%)
  local copies, waits for them, and re-layouts  5.96 us (6%)
    pallas_call x1, Pallas kernels, local(): pl.pallas_call(functools.partial(fused, n_src, n_loop, slots), out_shape=...  86 us
    unnamed x2, local copies, waits for them, and re-layouts  2.57 us

profile of v1, /device:TPU:0, one launch (start us, length us, event | category | flops | bytes accessed | tf_op | source)
XLA Modules:
  0.0 92.8 jit_solution(2939154583595959867)
XLA Ops:
  0.6 0.8 copy.9
  1.4 0.1 broadcast_subtract_fusion
  1.5 0.7 copy.10
  2.2 0.1 pad_add_fusion
  2.3 0.6 pad.4
  2.9 1.3 %reshape.8.g_old_ref = f32[8,1,512]{2,1,0:T(1,128)} reshape(bf16[8,512]{1,0:T(8,128)(2,1)} %param.10) | data formatting | bytes 24576 | tf_op jit(solution)/shard_map/broadcast_in_dim | solution.py:412
  4.2 86.0 %shard_map.86 = (f32[1,512]{1,0:T(1,128)}, f32[8,512]{1,0:T(8,128)}) custom-call(bf16[512,768]{1,0:T(8,128)(2,1)} %src_ref.1, bf16[8,512,768]{2,1,0:T(8,128)(2,1)} %tgt_ref.1, f32[1,512]{1,0:T(1,128)} %bitcast.9, f32[8,1,512]{2,1,0:T(1,128)} %reshape.8.g_old_ref, f32[8,512]{1,0:T(8,128)} %log_b_ref.1, s32[8,1,128]{2,1,0:T(1,128)} %bitcast.5), custom_call_target="tpu_custom_call" | custom-call | flops 6442450944 | bytes 7077888 | tf_op jit(solution)/shard_map/pallas_call | solution.py:366
  90.2 1.2 %copy.13 = f32[512]{0:T(512)} copy(f32[512]{0:T(512)} %bitcast.6) | data formatting | bytes 4096
  91.5 1.3 %copy.14 = f32[8,512]{1,0:T(8,128)} copy(f32[8,512]{1,0:T(8,128)} %get-tuple-element.9) | data formatting | bytes 32768
  (1 shorter events, 0.0 us)

commit v2 on v1

--- a/solution.py
+++ b/solution.py
@@ -18,9 +18,9 @@
 
 def fused(
     n_src, n_loop, slots,
-    src_ref, tgt_ref, log_a_ref, g_old_ref, log_b_ref, idpack_ref,
+    src_ref, tgt_ref, log_a_ref, g_old_ref, log_b_ref, list_ref, live_ref,
     f_ref, g_ref,
-    gather, tiles, logits, gcol, ids_v, ids_s, row_out, row_in, f_all,
+    gather, tiles, logits, gcol, idpack_ref, ids_v, ids_s, row_out, row_in, f_all,
     col_top, col_sum, loop_out, loop_in,
     gs_send, gs_recv, id_send, id_recv, row_send, row_recv, f_send, f_recv,
     loop_send, loop_recv, loc_sem,
@@ -47,10 +47,16 @@
 
     tile_copy = pltpu.make_async_copy(tgt_ref, tiles, loc_sem.at[0])
     own_copy = pltpu.make_async_copy(src_ref, gather.at[me], loc_sem.at[1])
-    own_ids = pltpu.make_async_copy(idpack_ref.at[me], ids_v.at[me], loc_sem.at[2])
     tile_copy.start()
     own_copy.start()
-    own_ids.start()
+
+    spot = lax.broadcasted_iota(jnp.int32, (1, 128), 1)
+    for s in range(n_src):
+        row = jnp.where(spot == slots, live_ref[0, s], 0)
+        for c in range(slots):
+            row = jnp.where(spot == c, lax.rem(list_ref[0, c, s], tiles_own), row)
+        idpack_ref[s] = row
+    ids_v[me] = idpack_ref[me]
 
     barrier = pltpu.get_barrier_semaphore()
     for k in range(1, n_src):
@@ -101,14 +107,11 @@
     for ch in range(CHUNKS):
         own_send(ch, 2, sib).start()
 
-    def fill(t, carry):
-        row = g_old_ref[t] * (LOG2E / EPSILON)
+    g_old = g_old_ref[...].astype(jnp.float32)
+    for t in range(tiles_own):
+        row = g_old[t : t + 1] * (LOG2E / EPSILON)
         gcol[t] = jnp.broadcast_to(row, (128, width)).T
-        return carry
-
-    lax.fori_loop(0, tiles_own, fill, 0)
-
-    own_ids.wait()
+
     for k in range(1, n_src):
         id_copy(peer(k), peer(k)).wait_recv()
     to_smem = pltpu.make_async_copy(ids_v, ids_s, loc_sem.at[3])
@@ -166,7 +169,7 @@
     lax.fori_loop(0, CHUNKS, sib_step, 0)
     row_copy(sib, me).start()
 
-    def chip_step(k, carry):
+    def chip_chunks(k, first, last):
         low = chip - k
         high = chip + k
 
@@ -215,18 +218,13 @@
 
             return lax.fori_loop(0, 4, part_step, carry)
 
-        return lax.fori_loop(0, CHUNKS, chunk_step, carry)
-
-    lax.fori_loop(1, n_chip, chip_step, 0)
-
-    for k in range(1, n_src):
-        row_copy(peer(k), peer(k)).wait_recv()
-    tops = row_in[:, 0, :]
-    best = jnp.max(tops, axis=0, keepdims=True)
-    total = jnp.sum(row_in[:, 1, :] * jnp.exp2(tops - best), axis=0, keepdims=True)
-    f_two = log_a_ref[...] * LOG2E - (best + jnp.log2(total))
-    f_ref[...] = f_two * (EPSILON * LN2)
-    f_all[me] = f_two
+        lax.fori_loop(first, last, chunk_step, 0)
+
+    def chip_step(k, carry):
+        chip_chunks(k, 0, CHUNKS)
+        return carry
+
+    lax.fori_loop(1, n_chip - 1, chip_step, 0)
 
     def f_copy(to, slot):
         return pltpu.make_async_remote_copy(
@@ -235,35 +233,73 @@
             device_id=at_src(to), device_id_type=MESH,
         )
 
-    for k in range(1, n_src):
-        f_copy(peer(k), me).start()
-    for k in range(1, n_src):
-        f_copy(peer(k), peer(k)).wait_recv()
+    def potential():
+        for k in range(1, n_src):
+            row_copy(peer(k), peer(k)).wait_recv()
+        tops = row_in[:, 0, :]
+        best = jnp.max(tops, axis=0, keepdims=True)
+        total = jnp.sum(row_in[:, 1, :] * jnp.exp2(tops - best), axis=0, keepdims=True)
+        f_two = log_a_ref[...] * LOG2E - (best + jnp.log2(total))
+        f_ref[...] = f_two * (EPSILON * LN2)
+        f_all[me] = f_two
+        for k in range(1, n_src):
+            f_copy(peer(k), me).start()
+
+    def wait_potential(blocks):
+        for s in blocks:
+            @pl.when(me != s)
+            def _():
+                f_copy(sib, s).wait_recv()
 
     n_pairs = n_src * slots
     band = 32
     lane = lax.broadcasted_iota(jnp.int32, (band, 128), 1)
 
-    def band_step(r, carry):
-        at = pl.ds(pl.multiple_of(r * band, band), band)
-
-        def pair_step(p, state):
-            tops, sums = state
-            vals = logits[p, at, :] + f_all[p // slots]
-            parts = [vals[:, i : i + 128] for i in range(0, rows, 128)]
-            top = functools.reduce(jnp.maximum, parts)
-            total = functools.reduce(jnp.add, [jnp.exp2(v - top) for v in parts])
-            full = jnp.max(top, axis=1, keepdims=True)
-            total = jnp.sum(total * jnp.exp2(top - full), axis=1, keepdims=True)
-            return (jnp.where(lane == p, full, tops), jnp.where(lane == p, total, sums))
-
-        zero = jnp.zeros((band, 128), jnp.float32)
-        tops, sums = lax.fori_loop(0, n_pairs, pair_step, (zero, zero), unroll=4)
-        col_top[at, :] = tops
-        col_sum[at, :] = sums
-        return carry
-
-    lax.fori_loop(0, width // band, band_step, 0)
+    def columns(count, pair_of, fresh):
+        def band_step(r, carry):
+            at = pl.ds(pl.multiple_of(r * band, band), band)
+
+            def pair_step(i, state):
+                tops, sums = state
+                p = pair_of(i)
+                vals = logits[p, at, :] + f_all[p // slots]
+                parts = [vals[:, i : i + 128] for i in range(0, rows, 128)]
+                top = functools.reduce(jnp.maximum, parts)
+                total = functools.reduce(jnp.add, [jnp.exp2(v - top) for v in parts])
+                full = jnp.max(top, axis=1, keepdims=True)
+                total = jnp.sum(total * jnp.exp2(top - full), axis=1, keepdims=True)
+                return (jnp.where(lane == p, full, tops), jnp.where(lane == p, total, sums))
+
+            if fresh:
+                state = (jnp.zeros((band, 128), jnp.float32),) * 2
+            else:
+                state = (col_top[at, :], col_sum[at, :])
+            tops, sums = lax.fori_loop(0, count, pair_step, state, unroll=4)
+            col_top[at, :] = tops
+            col_sum[at, :] = sums
+            return carry
+
+        lax.fori_loop(0, width // band, band_step, 0)
+
+    inner = (chip > 0) & (chip < n_chip - 1)
+    outer = jnp.logical_not(inner)
+    edge = 2 * slots
+    pl.when(inner)(potential)
+
+    @pl.when(outer)
+    def _():
+        chip_chunks(n_chip - 1, 0, CHUNKS - 1)
+
+    wait_potential(range(2, n_src - 2))
+    columns(n_pairs - 2 * edge, lambda i: i + edge, True)
+
+    @pl.when(outer)
+    def _():
+        chip_chunks(n_chip - 1, CHUNKS - 1, CHUNKS)
+        potential()
+
+    wait_potential([0, 1, n_src - 2, n_src - 1])
+    columns(2 * edge, lambda i: i + (i // edge) * (n_pairs - 2 * edge), False)
     tops = col_top[...].T
     sums = col_sum[...].T
     index = lax.broadcasted_iota(jnp.int32, (tiles_own, width), 0)
@@ -301,7 +337,7 @@
         jnp.add, [loop_in[i, 1] * jnp.exp2(loop_in[i, 0] - top) for i in range(n_loop)]
     )
     g_ref[...] = (
-        EPSILON * log_b_ref[...] - (EPSILON * LN2) * (top + jnp.log2(total)) + g_old_ref[:, 0, :]
+        EPSILON * log_b_ref[...] - (EPSILON * LN2) * (top + jnp.log2(total)) + g_old
     )
 
     for k in range(1, n_loop):
@@ -356,11 +392,9 @@
     rows, depth = sources.shape
     tiles_own, width = targets.shape[0], targets.shape[1]
     slots = tile_ids.shape[2]
-    base = jnp.arange(n_src, dtype=jnp.int32) * tiles_own
-    listed = jnp.concatenate([tile_ids[0] - base[:, None], live_count[0][:, None]], axis=1)
-    idpack = jnp.pad(listed, ((0, 0), (0, 128 - slots - 1)))[:, None, :]
     vmem = pl.BlockSpec(memory_space=pltpu.VMEM)
     hbm = pl.BlockSpec(memory_space=pl.ANY)
+    smem = pl.BlockSpec(memory_space=pltpu.SMEM)
     dma = pltpu.SemaphoreType.DMA
     n_pairs = n_src * slots
     f_new, g_new = pl.pallas_call(
@@ -369,13 +403,14 @@
             jax.ShapeDtypeStruct((1, rows), jnp.float32),
             jax.ShapeDtypeStruct((tiles_own, width), jnp.float32),
         ),
-        in_specs=[hbm, hbm, vmem, vmem, vmem, vmem],
+        in_specs=[hbm, hbm, vmem, vmem, vmem, smem, smem],
         out_specs=(vmem, vmem),
         scratch_shapes=[
             pltpu.VMEM((n_src, rows, depth), sources.dtype),
             pltpu.VMEM((tiles_own, width, depth), targets.dtype),
             pltpu.VMEM((n_pairs, width, rows), jnp.float32),
             pltpu.VMEM((tiles_own, width, 128), jnp.float32),
+            pltpu.VMEM((n_src, 1, 128), jnp.int32),
             pltpu.VMEM((n_src, 1, 128), jnp.int32),
             pltpu.SMEM((n_src, 1, 128), jnp.int32),
             pltpu.VMEM((n_src, 2, rows), jnp.float32),
@@ -409,9 +444,10 @@
         sources,
         targets,
         log_a[None],
-        g_old.astype(jnp.float32)[:, None, :],
+        g_old,
         log_b,
-        idpack,
+        jnp.swapaxes(tile_ids, 1, 2),
+        live_count,
     )
     return (f_new[0], g_new)
 

time: 93.2 us -> 90.3 us (0.969)
  local copies, waits for them, and re-layouts: 5.96 us -> 2.55 us
    broadcast_in_dim x1 -> x0, local copies, waits for them, and re-layouts: 1.31 us -> none  [local(): g_old.astype(jnp.float32)[:, None, :]]
where the time goes in v2:
time: 90.3 us; the launch traced here: 90 us
  Pallas kernels  86.8 us (96%)
  local copies, waits for them, and re-layouts  2.55 us (3%)
    pallas_call x1, Pallas kernels, local(): pl.pallas_call(functools.partial(fused, n_src, n_loop, slots), out_shape=...  86.8 us
    unnamed x2, local copies, waits for them, and re-layouts  2.55 us

profile of v2, /device:TPU:0, one launch (start us, length us, event | category | flops | bytes accessed | tf_op | source)
XLA Modules:
  0.0 90.0 jit_solution(36595730011120565)
XLA Ops:
  0.6 86.8 %shard_map.86 = (f32[1,512]{1,0:T(1,128)}, f32[8,512]{1,0:T(8,128)}) custom-call(bf16[512,768]{1,0:T(8,128)(2,1)} %src_ref.1, bf16[8,512,768]{2,1,0:T(8,128)(2,1)} %tgt_ref.1, f32[1,512]{1,0:T(1,128)} %bitcast.4, bf16[8,512]{1,0:T(8,128)(2,1)} %g_old_ref.1, f32[8,512]{1,0:T(8,128)} %log_b_ref.1, s32[1,2,8]{2,1,0:T(2,128)} %bitcast.5, s32[1,8]{1,0:T(1,128)} %live_ref.1), custom_call_target="tpu_custom_call" | custom-call | flops 6442450944 | bytes 7077888 | tf_op jit(solution)/shard_map/pallas_call | solution.py:400
  87.5 1.2 %copy.11 = f32[512]{0:T(512)} copy(f32[512]{0:T(512)} %bitcast.3) | data formatting | bytes 4096
  88.7 1.3 %copy.12 = f32[8,512]{1,0:T(8,128)} copy(f32[8,512]{1,0:T(8,128)} %get-tuple-element.9) | data formatting | bytes 32768

commit v3 on v2

--- a/solution.py
+++ b/solution.py
@@ -12,7 +12,7 @@
 VERY_LOW = -1e30
 LOG2E = math.log2(math.e)
 LN2 = math.log(2.0)
-CHUNKS = 2
+CHUNKS = 4
 MESH = pl.DeviceIdType.MESH
 
 
@@ -384,6 +384,11 @@
         return carry
 
     lax.fori_loop(1, n_chip, drain, 0)
+
+
+def hand_on(f_in, g_in, f_ref, g_ref):
+    f_ref[...] = f_in[...]
+    g_ref[...] = g_in[...]
 
 
 def local(sources, log_a, targets, g_old, log_b, tile_ids, live_count):
@@ -449,6 +454,15 @@
         jnp.swapaxes(tile_ids, 1, 2),
         live_count,
     )
+    f_new, g_new = pl.pallas_call(
+        hand_on,
+        out_shape=(
+            jax.ShapeDtypeStruct((1, rows), jnp.float32),
+            jax.ShapeDtypeStruct((tiles_own, width), jnp.float32),
+        ),
+        in_specs=[vmem, vmem],
+        out_specs=(vmem, vmem),
+    )(f_new, g_new)
     return (f_new[0], g_new)
 
 

time: 90.3 us -> 89.3 us (0.989)
  local copies, waits for them, and re-layouts: 2.55 us -> 0 us
  Pallas kernels: 86.8 us -> 88.4 us
    unnamed x2 -> x0, local copies, waits for them, and re-layouts: 2.55 us -> none
    pallas_call x0 -> x1, Pallas kernels: none -> 1.33 us  [local(): pl.pallas_call(hand_on, out_shape=(jax.ShapeDtypeStruct((1, rows), jnp.fl...]
where the time goes in v3:
time: 89.3 us; the launch traced here: 89 us
  Pallas kernels  88.4 us (99%)
    pallas_call x1, Pallas kernels, local(): pl.pallas_call(functools.partial(fused, n_src, n_loop, slots), out_shape=...  87.1 us

profile of v3, /device:TPU:0, one launch (start us, length us, event | category | flops | bytes accessed | tf_op | source)
XLA Modules:
  0.0 89.0 jit_solution(589123135611677737)
XLA Ops:
  0.6 87.1 %shard_map.86 = (f32[1,512]{1,0:T(1,128)}, f32[8,512]{1,0:T(8,128)}) custom-call(bf16[512,768]{1,0:T(8,128)(2,1)} %src_ref.1, bf16[8,512,768]{2,1,0:T(8,128)(2,1)} %tgt_ref.1, f32[1,512]{1,0:T(1,128)} %bitcast.3, bf16[8,512]{1,0:T(8,128)(2,1)} %g_old_ref.1, f32[8,512]{1,0:T(8,128)} %log_b_ref.1, s32[1,2,8]{2,1,0:T(2,128)} %bitcast.5, s32[1,8]{1,0:T(1,128)} %live_ref.1), custom_call_target="tpu_custom_call" | custom-call | flops 6442450944 | bytes 7077888 | tf_op jit(solution)/shard_map/pallas_call | solution.py:405
  87.7 1.3 %shard_map.87 = (f32[1,512]{1,0:T(1,128)}, f32[8,512]{1,0:T(8,128)}) custom-call(f32[1,512]{1,0:T(1,128)} %get-tuple-element.6.f_in, f32[8,512]{1,0:T(8,128)} %get-tuple-element.7.g_in), custom_call_target="tpu_custom_call" | custom-call | tf_op jit(solution)/shard_map/pallas_call | solution.py:457

commit v4 on v3

--- a/solution.py
+++ b/solution.py
@@ -12,7 +12,7 @@
 VERY_LOW = -1e30
 LOG2E = math.log2(math.e)
 LN2 = math.log(2.0)
-CHUNKS = 4
+CHUNKS = 2
 MESH = pl.DeviceIdType.MESH
 
 
@@ -274,7 +274,7 @@
                 state = (jnp.zeros((band, 128), jnp.float32),) * 2
             else:
                 state = (col_top[at, :], col_sum[at, :])
-            tops, sums = lax.fori_loop(0, count, pair_step, state, unroll=4)
+            tops, sums = lax.fori_loop(0, count, pair_step, state, unroll=8)
             col_top[at, :] = tops
             col_sum[at, :] = sums
             return carry

time: 89.3 us -> 83.3 us (0.933)
  Pallas kernels: 88.4 us -> 82.5 us
    pallas_call x1, Pallas kernels: 87.1 us -> 81.1 us  [local(): pl.pallas_call(functools.partial(fused, n_src, n_loop, slots), out_shape=...]
where the time goes in v4:
time: 83.3 us; the launch traced here: 83.1 us
  Pallas kernels  82.5 us (99%)
    pallas_call x1, Pallas kernels, local(): pl.pallas_call(functools.partial(fused, n_src, n_loop, slots), out_shape=...  81.1 us

profile of v4, /device:TPU:0, one launch (start us, length us, event | category | flops | bytes accessed | tf_op | source)
XLA Modules:
  0.0 83.1 jit_solution(2945065739709787432)
XLA Ops:
  0.6 81.1 %shard_map.86 = (f32[1,512]{1,0:T(1,128)}, f32[8,512]{1,0:T(8,128)}) custom-call(bf16[512,768]{1,0:T(8,128)(2,1)} %src_ref.1, bf16[8,512,768]{2,1,0:T(8,128)(2,1)} %tgt_ref.1, f32[1,512]{1,0:T(1,128)} %bitcast.3, bf16[8,512]{1,0:T(8,128)(2,1)} %g_old_ref.1, f32[8,512]{1,0:T(8,128)} %log_b_ref.1, s32[1,2,8]{2,1,0:T(2,128)} %bitcast.5, s32[1,8]{1,0:T(1,128)} %live_ref.1), custom_call_target="tpu_custom_call" | custom-call | flops 6442450944 | bytes 7077888 | tf_op jit(solution)/shard_map/pallas_call | solution.py:405
  81.8 1.3 %shard_map.87 = (f32[1,512]{1,0:T(1,128)}, f32[8,512]{1,0:T(8,128)}) custom-call(f32[1,512]{1,0:T(1,128)} %get-tuple-element.6.f_in, f32[8,512]{1,0:T(8,128)} %get-tuple-element.7.g_in), custom_call_target="tpu_custom_call" | custom-call | tf_op jit(solution)/shard_map/pallas_call | solution.py:457
